TPU v7x, 32 devices: a whole 2x2x4 slice. The times are simulated.
32 devices in a mesh: section: 2 (over core), ctx: 4 (over y, x), wshard: 4 (over z).
Axes of the slice: x: 2, y: 2, z: 4, core: 2. Of those that a mesh axis runs over, the one named last changes fastest.
Arguments:
- tokens: bfloat16 [8, 1024, 768], P('wshard', 'ctx'), may hold values from -6 to 6
- cotangent: bfloat16 [8, 1024, 768], P('wshard', 'ctx'), may hold values from -6 to 6
- block_map: int32 [8, 8], P('wshard'), may hold values from 0 to 7, each once within a row
- w_qkv: bfloat16 [2, 768, 2304], P('section', 'wshard'), may hold values from -0.21875 to 0.21875
- b_qkv: bfloat16 [2, 2304], P('section', 'wshard'), may hold values from -3 to 3
- w_out: bfloat16 [2, 768, 768], P('section', 'wshard'), may hold values from -1.75 to 1.75
- b_out: bfloat16 [2, 768], P('section', 'wshard'), may hold values from -3 to 3
- w_up: bfloat16 [2, 768, 3072], P('section', 'wshard'), may hold values from -0.21875 to 0.21875
- b_up: bfloat16 [2, 3072], P('section', 'wshard'), may hold values from -3 to 3
- w_down: bfloat16 [2, 3072, 768], P('section', 'wshard'), may hold values from -0.109375 to 0.109375
- b_down: bfloat16 [2, 768], P('section', 'wshard'), may hold values from -3 to 3
- gain_attn: bfloat16 [2, 768], P('section', 'wshard'), may hold values from 0.5 to 1.5
- shift_attn: bfloat16 [2, 768], P('section', 'wshard'), may hold values from -2 to 2
- gain_mlp: bfloat16 [2, 768], P('section', 'wshard'), may hold values from 0.5 to 1.5
- shift_mlp: bfloat16 [2, 768], P('section', 'wshard'), may hold values from -2 to 2
Outputs:
- layer_outputs: bfloat16 [2, 8, 1024, 768], P('section', 'wshard', 'ctx')
- boundary_grads: float32 [2, 8, 1024, 768], P('section', 'wshard', 'ctx')
- grad_w_qkv: float32 [2, 768, 2304], P('section', 'wshard')
- grad_b_qkv: float32 [2, 2304], P('section', 'wshard')
- grad_w_out: float32 [2, 768, 768], P('section', 'wshard')
- grad_b_out: float32 [2, 768], P('section', 'wshard')
- grad_w_up: float32 [2, 768, 3072], P('section', 'wshard')
- grad_b_up: float32 [2, 3072], P('section', 'wshard')
- grad_w_down: float32 [2, 3072, 768], P('section', 'wshard')
- grad_b_down: float32 [2, 768], P('section', 'wshard')
- grad_gain_attn: float32 [2, 768], P('section', 'wshard')
- grad_shift_attn: float32 [2, 768], P('section', 'wshard')
- grad_gain_mlp: float32 [2, 768], P('section', 'wshard')
- grad_shift_mlp: float32 [2, 768], P('section', 'wshard')
Inputs may be any that keep to these rules, and one draw needn't show every extreme that they name: Each row is an order of the 8 blocks of 128 tokens of one sequence: stored slot i holds block block_map[s, i], and each block stands in one slot.
All inputs are finite; a program needn't handle non-finite values.
Results may differ from a plain program's by a relative error of at most 0.015.
Values may be sent and summed in bfloat16 or wider, within the bound.
A program may use at most 320 MiB of HBM per device.

v0:
```python
from functools import partial
import math

import jax
import jax.numpy as jnp
from jax import lax
from jax.sharding import PartitionSpec as P

D = 768
H = 12
HD = 64
FF = 3072
ROT = 16


EPSILON = 1e-05


def passed_along(shard, axis, by):
    count = lax.axis_size(axis)
    pairs = [(i, i + by) for i in range(count) if 0 <= i + by < count]
    return lax.ppermute(shard, axis, pairs)


def shortened(shard):

    def short(part):
        return part.astype(jnp.bfloat16) if part.dtype == jnp.float32 else part

    return jax.tree.map(short, shard)


def layer_norm(values, gain_vec, shift_vec):
    center = values - jnp.mean(values, axis=-1, keepdims=True)
    spread = jnp.mean(center * center, axis=-1, keepdims=True)
    return center * lax.rsqrt(spread + EPSILON) * gain_vec + shift_vec


def angles(places, rot_width):
    half_width = rot_width // 2
    frequency = jnp.exp(
        jnp.arange(half_width, dtype=jnp.float32)
        * jnp.float32(-2.0 * math.log(10000.0) / rot_width)
    )
    return places.astype(jnp.float32)[:, None] * frequency[None, :]


def rotate(tensor, turn_angle, rotation_sign):
    half_width = turn_angle.shape[-1]
    cosine = jnp.cos(turn_angle)[:, None, :]
    sine_term = rotation_sign * jnp.sin(turn_angle)[:, None, :]
    lower_half = tensor[..., :half_width]
    upper_half = tensor[..., half_width : 2 * half_width]
    return jnp.concatenate(
        [
            lower_half * cosine - upper_half * sine_term,
            upper_half * cosine + lower_half * sine_term,
            tensor[..., 2 * half_width :],
        ],
        axis=-1,
    )


def positions(order_row, block_rows):
    return jnp.repeat(order_row, block_rows) * block_rows + jnp.tile(
        jnp.arange(block_rows, dtype=jnp.int32), order_row.shape[0]
    )


def own_places(order_row, row_count):
    places_all = positions(order_row, row_count // 2)
    places_own = lax.dynamic_slice_in_dim(places_all, lax.axis_index("ctx") * row_count, row_count)
    return (places_all, places_own)


def layer_state(current, weights, order_row):
    (
        w_qkv,
        b_qkv,
        w_out,
        b_out,
        w_up,
        b_up,
        w_down,
        b_down,
        gain_attn,
        shift_attn,
        gain_mlp,
        shift_mlp,
    ) = weights
    row_count = current.shape[0]
    places_all, places_own = own_places(order_row, row_count)
    turn_angle = angles(places_own, ROT)
    normed_a = layer_norm(current, gain_attn, shift_attn).astype(jnp.bfloat16)
    normed_m = layer_norm(current, gain_mlp, shift_mlp).astype(jnp.bfloat16)
    projected = jnp.dot(normed_a, w_qkv, preferred_element_type=jnp.float32) + b_qkv
    queries = rotate(projected[:, :D].reshape(row_count, H, HD), turn_angle, 1.0).astype(
        jnp.bfloat16
    )
    key_rows = (
        rotate(projected[:, D : 2 * D].reshape(row_count, H, HD), turn_angle, 1.0)
        .reshape(row_count, D)
        .astype(jnp.bfloat16)
    )
    value_rows = projected[:, 2 * D :].astype(jnp.bfloat16)
    all_keys, all_values = (
        lax.all_gather(key_rows, "ctx", axis=0, tiled=True),
        lax.all_gather(value_rows, "ctx", axis=0, tiled=True),
    )
    all_keys = all_keys.reshape(-1, H, HD)
    all_values = all_values.reshape(-1, H, HD)
    scores = (
        jnp.einsum("qhd,khd->hqk", queries, all_keys, preferred_element_type=jnp.float32) * 0.125
    )
    visible = places_all[None, :] <= places_own[:, None]
    masked = jnp.where(visible[None], scores, -1e30)
    attn_probs = jax.nn.softmax(masked, axis=-1)
    log_total = jax.nn.logsumexp(masked, axis=-1)
    probs_low = attn_probs.astype(jnp.bfloat16)
    mixed_heads = (
        jnp.einsum("hqk,khd->qhd", probs_low, all_values, preferred_element_type=jnp.float32)
        .reshape(row_count, D)
        .astype(jnp.bfloat16)
    )
    attn_branch = jnp.dot(mixed_heads, w_out, preferred_element_type=jnp.float32) + b_out
    pre_act = jnp.dot(normed_m, w_up, preferred_element_type=jnp.float32) + b_up
    active = jax.nn.gelu(pre_act, approximate=False).astype(jnp.bfloat16)
    mlp_branch = jnp.dot(active, w_down, preferred_element_type=jnp.float32) + b_down
    result = (current + attn_branch + mlp_branch).astype(jnp.bfloat16)
    return (
        result,
        (
            normed_a,
            normed_m,
            queries,
            all_keys,
            all_values,
            mixed_heads,
            pre_act,
            active,
            turn_angle,
            log_total,
        ),
    )


def layer_back(current, weights, order_row, grad_out, kept):
    (
        w_qkv,
        b_qkv,
        w_out,
        b_out,
        w_up,
        b_up,
        w_down,
        b_down,
        gain_attn,
        shift_attn,
        gain_mlp,
        shift_mlp,
    ) = weights
    row_count = current.shape[0]
    (
        normed_a,
        normed_m,
        queries,
        all_keys,
        all_values,
        mixed_heads,
        pre_act,
        active,
        turn_angle,
        log_total,
    ) = kept
    places_all, places_own = own_places(order_row, row_count)
    scores = (
        jnp.einsum("qhd,khd->hqk", queries, all_keys, preferred_element_type=jnp.float32) * 0.125
    )
    visible = places_all[None, :] <= places_own[:, None]
    attn_probs = jnp.where(visible[None], jnp.exp(scores - log_total[:, :, None]), 0.0)
    probs_low = attn_probs.astype(jnp.bfloat16)
    grad_low = grad_out.astype(jnp.bfloat16)
    grad_bias = jnp.sum(grad_out, axis=0)
    grad_mixed = (
        jnp.einsum("re,de->rd", grad_low, w_out, preferred_element_type=jnp.float32)
        .astype(jnp.bfloat16)
        .reshape(row_count, H, HD)
    )
    grad_probs = jnp.einsum(
        "qhd,khd->hqk", grad_mixed, all_values, preferred_element_type=jnp.float32
    )
    row_delta = jnp.sum(attn_probs * grad_probs, axis=-1)
    grad_scores = attn_probs * (grad_probs - row_delta[:, :, None])
    scaled_low = grad_scores.astype(jnp.bfloat16) * 0.125
    grad_queries = jnp.einsum(
        "hqk,khd->qhd", scaled_low, all_keys, preferred_element_type=jnp.float32
    ).astype(jnp.bfloat16)
    key_terms = jnp.einsum(
        "hqk,qhd->khd", scaled_low, queries, preferred_element_type=jnp.float32
    ).reshape(-1, D)
    value_terms = jnp.einsum(
        "hqk,qhd->khd", probs_low, grad_mixed, preferred_element_type=jnp.float32
    ).reshape(-1, D)
    grad_keys, grad_values = (
        lax.psum_scatter(
            key_terms.astype(jnp.bfloat16), "ctx", scatter_dimension=0, tiled=True
        ).astype(jnp.float32),
        lax.psum_scatter(
            value_terms.astype(jnp.bfloat16), "ctx", scatter_dimension=0, tiled=True
        ).astype(jnp.float32),
    )
    key_rounded = grad_keys.astype(jnp.bfloat16).astype(jnp.float32).reshape(row_count, H, HD)
    query_raw = rotate(grad_queries.astype(jnp.float32), turn_angle, -1.0).reshape(row_count, D)
    key_raw = rotate(key_rounded, turn_angle, -1.0).reshape(row_count, D)
    grad_projected = jnp.concatenate([query_raw, key_raw, grad_values], axis=-1).astype(
        jnp.bfloat16
    )
    grad_b_qkv = jnp.sum(grad_projected.astype(jnp.float32), axis=0)
    grad_normed_a = jnp.einsum(
        "re,de->rd", grad_projected, w_qkv, preferred_element_type=jnp.float32
    )
    grad_active = jnp.einsum("re,fe->rf", grad_low, w_down, preferred_element_type=jnp.float32)
    unused_value, gelu_back = jax.vjp(partial(jax.nn.gelu, approximate=False), pre_act)
    grad_pre = gelu_back(grad_active)[0].astype(jnp.bfloat16)
    grad_b_up = jnp.sum(grad_pre.astype(jnp.float32), axis=0)
    grad_normed_m = jnp.einsum("rf,df->rd", grad_pre, w_up, preferred_element_type=jnp.float32)
    unused_attn, norm_back_attn = jax.vjp(
        layer_norm, current, gain_attn.astype(jnp.float32), shift_attn.astype(jnp.float32)
    )
    from_attn, grad_gain_attn, grad_shift_attn = norm_back_attn(grad_normed_a)
    unused_mlp, norm_back_mlp = jax.vjp(
        layer_norm, current, gain_mlp.astype(jnp.float32), shift_mlp.astype(jnp.float32)
    )
    from_mlp, grad_gain_mlp, grad_shift_mlp = norm_back_mlp(grad_normed_m)
    grad_input = (grad_out + from_attn + from_mlp).astype(jnp.bfloat16)
    operands = (normed_a, grad_projected, mixed_heads, grad_low, normed_m, grad_pre, active)
    small_sums = (
        grad_b_qkv,
        grad_bias,
        grad_b_up,
        grad_gain_attn,
        grad_shift_attn,
        grad_gain_mlp,
        grad_shift_mlp,
    )
    return (grad_input, operands, small_sums)


def pick_turn(stacked, index_value):
    return lax.dynamic_index_in_dim(stacked, index_value, 0, keepdims=False)


def per_device(
    tokens,
    cotangent,
    block_map,
    w_qkv,
    b_qkv,
    w_out,
    b_out,
    w_up,
    b_up,
    w_down,
    b_down,
    gain_attn,
    shift_attn,
    gain_mlp,
    shift_mlp,
):
    shards = (
        w_qkv,
        b_qkv,
        w_out,
        b_out,
        w_up,
        b_up,
        w_down,
        b_down,
        gain_attn,
        shift_attn,
        gain_mlp,
        shift_mlp,
    )
    first_section = lax.axis_index("section") == 0
    batches = tokens.shape[0]
    gathered = (
        lax.all_gather(shards[0], "wshard", axis=1, tiled=True),
        lax.all_gather(shards[1], "wshard", axis=1, tiled=True),
        lax.all_gather(shards[2], "wshard", axis=1, tiled=True),
        lax.all_gather(shards[3], "wshard", axis=1, tiled=True),
        lax.all_gather(shards[4], "wshard", axis=1, tiled=True),
        lax.all_gather(shards[5], "wshard", axis=1, tiled=True),
        lax.all_gather(shards[6], "wshard", axis=1, tiled=True),
        lax.all_gather(shards[7], "wshard", axis=1, tiled=True),
        lax.all_gather(shards[8], "wshard", axis=1, tiled=True),
        lax.all_gather(shards[9], "wshard", axis=1, tiled=True),
        lax.all_gather(shards[10], "wshard", axis=1, tiled=True),
        lax.all_gather(shards[11], "wshard", axis=1, tiled=True),
    )
    weights = tuple((whole_piece[0] for whole_piece in gathered))
    zero_rows = jnp.zeros(tokens.shape[1:], jnp.float32)
    turns = jnp.arange(batches + 1, dtype=jnp.int32)

    def forward_turn(arrived, turn):
        fresh_rows = jnp.where(
            turn < batches,
            pick_turn(tokens, jnp.minimum(turn, batches - 1)).astype(jnp.float32),
            0.0,
        )
        current = jnp.where(first_section, fresh_rows, arrived)
        order_row = jnp.where(
            first_section,
            pick_turn(block_map, jnp.minimum(turn, batches - 1)),
            pick_turn(block_map, jnp.maximum(turn - 1, 0)),
        )
        result, state_kept = layer_state(current, weights, order_row)
        sent = passed_along(result, "section", 1).astype(jnp.float32)
        return (sent, (current, order_row, state_kept, result))

    unused_arrived, (kept_inputs, kept_orders, kept_states, produced) = lax.scan(
        forward_turn, zero_rows, turns
    )
    regathered = (
        lax.all_gather(shards[0], "wshard", axis=1, tiled=True),
        lax.all_gather(shards[1], "wshard", axis=1, tiled=True),
        lax.all_gather(shards[2], "wshard", axis=1, tiled=True),
        lax.all_gather(shards[3], "wshard", axis=1, tiled=True),
        lax.all_gather(shards[4], "wshard", axis=1, tiled=True),
        lax.all_gather(shards[5], "wshard", axis=1, tiled=True),
        lax.all_gather(shards[6], "wshard", axis=1, tiled=True),
        lax.all_gather(shards[7], "wshard", axis=1, tiled=True),
        lax.all_gather(shards[8], "wshard", axis=1, tiled=True),
        lax.all_gather(shards[9], "wshard", axis=1, tiled=True),
        lax.all_gather(shards[10], "wshard", axis=1, tiled=True),
        lax.all_gather(shards[11], "wshard", axis=1, tiled=True),
    )
    weights = tuple((whole_piece[0] for whole_piece in regathered))

    def backward_turn(carry, turn):
        returned, small_totals = carry
        upstream = jnp.where(
            turn < batches,
            pick_turn(cotangent, jnp.minimum(turn, batches - 1)).astype(jnp.float32),
            0.0,
        )
        grad_out = jnp.where(first_section, returned, upstream)
        lower_turn = jnp.maximum(turn - 1, 0)
        upper_turn = jnp.minimum(turn + 1, batches)

        def choose(stacked):
            return jnp.where(
                first_section, pick_turn(stacked, lower_turn), pick_turn(stacked, upper_turn)
            )

        source = choose(kept_inputs)
        order_row = choose(kept_orders)
        state_used = jax.tree.map(choose, kept_states)
        grad_input, operands, small_sums = layer_back(
            source, weights, order_row, grad_out, state_used
        )
        small_totals = tuple((total + term for total, term in zip(small_totals, small_sums)))
        returned_next = passed_along(grad_input, "section", -1).astype(jnp.float32)
        return ((returned_next, small_totals), (operands, grad_input))

    start_sums = (
        jnp.zeros((3 * D,), jnp.float32),
        jnp.zeros((D,), jnp.float32),
        jnp.zeros((FF,), jnp.float32),
        jnp.zeros((D,), jnp.float32),
        jnp.zeros((D,), jnp.float32),
        jnp.zeros((D,), jnp.float32),
        jnp.zeros((D,), jnp.float32),
    )
    (unused_returned, small_totals), (operand_stacks, input_grads) = lax.scan(
        backward_turn, (zero_rows, start_sums), turns
    )
    joined = [stacked.reshape(-1, stacked.shape[-1]) for stacked in operand_stacks]
    (
        normed_a_rows,
        grad_projected_rows,
        mixed_rows,
        grad_low_rows,
        normed_m_rows,
        grad_pre_rows,
        active_rows,
    ) = joined
    grad_w_qkv = jnp.einsum(
        "rd,re->de", normed_a_rows, grad_projected_rows, preferred_element_type=jnp.float32
    )
    grad_w_out = jnp.einsum(
        "rd,re->de", mixed_rows, grad_low_rows, preferred_element_type=jnp.float32
    )
    grad_w_up = jnp.einsum(
        "rd,rf->df", normed_m_rows, grad_pre_rows, preferred_element_type=jnp.float32
    )
    grad_w_down = jnp.einsum(
        "rf,re->fe", active_rows, grad_low_rows, preferred_element_type=jnp.float32
    )
    (
        grad_b_qkv,
        grad_bias,
        grad_b_up,
        grad_gain_attn,
        grad_shift_attn,
        grad_gain_mlp,
        grad_shift_mlp,
    ) = small_totals
    totals = (
        grad_w_qkv,
        grad_b_qkv,
        grad_w_out,
        grad_bias,
        grad_w_up,
        grad_b_up,
        grad_w_down,
        grad_bias,
        grad_gain_attn,
        grad_shift_attn,
        grad_gain_mlp,
        grad_shift_mlp,
    )
    summed = jax.tree.map(
        lambda part: part.astype(jnp.float32),
        lax.psum_scatter(
            shortened(tuple((total[None] for total in totals))),
            "wshard",
            scatter_dimension=1,
            tiled=True,
        ),
    )
    complete = jax.tree.map(
        lambda part: part.astype(jnp.float32), lax.psum(shortened(summed), "ctx")
    )
    outputs = jnp.where(first_section, produced[:batches], produced[1:])[None]
    boundary = jnp.where(first_section, input_grads[1:], input_grads[:batches]).astype(jnp.float32)[
        None
    ]
    return (
        outputs,
        boundary,
        complete[0],
        complete[1],
        complete[2],
        complete[3],
        complete[4],
        complete[5],
        complete[6],
        complete[7],
        complete[8],
        complete[9],
        complete[10],
        complete[11],
    )


def solution(mesh):
    in_specs = (
        P("wshard", "ctx", None),
        P("wshard", "ctx", None),
        P("wshard", None),
        P("section", "wshard", None),
        P("section", "wshard"),
        P("section", "wshard", None),
        P("section", "wshard"),
        P("section", "wshard", None),
        P("section", "wshard"),
        P("section", "wshard", None),
        P("section", "wshard"),
        P("section", "wshard"),
        P("section", "wshard"),
        P("section", "wshard"),
        P("section", "wshard"),
    )
    out_specs = (
        P("section", "wshard", "ctx", None),
        P("section", "wshard", "ctx", None),
        P("section", "wshard", None),
        P("section", "wshard"),
        P("section", "wshard", None),
        P("section", "wshard"),
        P("section", "wshard", None),
        P("section", "wshard"),
        P("section", "wshard", None),
        P("section", "wshard"),
        P("section", "wshard"),
        P("section", "wshard"),
        P("section", "wshard"),
        P("section", "wshard"),
    )
    return jax.shard_map(
        per_device, mesh=mesh, in_specs=in_specs, out_specs=out_specs, check_vma=False
    )
```

profile of v0, /device:TPU:0, one launch (start us, length us, event | category | flops | bytes accessed | tf_op | source)
XLA Modules:
  0.0 1600.0 jit_solution(4038889687839849144)
XLA Ops:
  29.3 20.0 %all-reduce.7 = (bf16[768]{0:T(1024)(128)(2,1)}, bf16[768]{0:T(1024)(128)(2,1)}, bf16[2304]{0:T(1024)(128)(2,1)}, bf16[768]{0:T(1024)(128)(2,1)}, bf16[768]{0:T(...) all-reduce(bf16[768]{0:T(1024)(128)(2,1)S(1)} %dynamic-update-slice, ...), channel_id=1, replica_groups=mesh['section'=2,'ctx'=4,'wshard'=4] {'wshard'}, use_global_device_ids=true, to_apply=%add | all-reduce | flops 6912 | bytes 27648 | tf_op jit(solution)/shard_map/squeeze | solution.py:300
  49.3 65.3 %all-gather.7.cloned.1.call-done = bf16[1,768,2304]{2,1,0:T(8,128)(2,1)} async-done(((bf16[1,192,2304]{2,1,0:T(8,128)(2,1)}), bf16[1,768,2304]{2,1,0:T(8,128)(2,1)}) %all-gather.7.cloned.1.call-update) | async-done | bytes 3538960 | tf_op jit(solution)/shard_map/all_gather | solution.py:287
  114.6 89.6 %all-gather.11.cloned.1.call-done = bf16[1,768,3072]{2,1,0:T(8,128)(2,1)} async-done(((bf16[1,192,3072]{2,1,0:T(8,128)(2,1)}), bf16[1,768,3072]{2,1,0:T(8,128)(2,1)}) %all-gather.11.cloned.1.call-update) | async-done | bytes 4718608 | tf_op jit(solution)/shard_map/all_gather | solution.py:291
  204.2 89.3 %all-gather.13.cloned.1.call-done = bf16[1,3072,768]{2,1,0:T(8,128)(2,1)} async-done(((bf16[1,768,768]{2,1,0:T(8,128)(2,1)}), bf16[1,3072,768]{2,1,0:T(8,128)(2,1)}) %all-gather.13.cloned.1.call-update) | async-done | bytes 4718608 | tf_op jit(solution)/shard_map/all_gather | solution.py:293
  301.2 307.3 %while.82 = (s32[]{:T(128)}, f32[256,768]{1,0:T(8,128)S(1)}, f32[3,256,768]{2,1,0:T(8,128)}, s32[3,8]{1,0:T(4,128)}, bf16[3,256,768]{2,1,0:T(8,128)(2,1)}, /*ind...) while((s32[]{:T(128)}, f32[256,768]{1,0:T(8,128)S(1)}, ...), condition=%wide.region_6.7_spmd.clone, body=%wide.region_0.6_spmd.clone.sunk | while | flops 4536426496 | bytes 186928592 | solution.py:320
  365.3 19.1 %all-gather.15.cloned.1.call-done = bf16[1024,768]{1,0:T(8,128)(2,1)} async-done(((bf16[256,768]{1,0:T(8,128)(2,1)}), bf16[1024,768]{1,0:T(8,128)(2,1)}) %all-gather.15.cloned.1.call-update) | async-done | bytes 1572880 | tf_op jit(solution)/shard_map/while/body/eval_jaxpr/all_gather | solution.py:108
  468.1 19.3 %all-gather.15.cloned.1.call-done = bf16[1024,768]{1,0:T(8,128)(2,1)} async-done(((bf16[256,768]{1,0:T(8,128)(2,1)}), bf16[1024,768]{1,0:T(8,128)(2,1)}) %all-gather.15.cloned.1.call-update) | async-done | bytes 1572880 | tf_op jit(solution)/shard_map/while/body/eval_jaxpr/all_gather | solution.py:108
  571.1 19.1 %all-gather.15.cloned.1.call-done = bf16[1024,768]{1,0:T(8,128)(2,1)} async-done(((bf16[256,768]{1,0:T(8,128)(2,1)}), bf16[1024,768]{1,0:T(8,128)(2,1)}) %all-gather.15.cloned.1.call-update) | async-done | bytes 1572880 | tf_op jit(solution)/shard_map/while/body/eval_jaxpr/all_gather | solution.py:108
  620.1 440.8 %while.83 = (s32[]{:T(128)}, f32[256,768]{1,0:T(8,128)S(1)}, f32[2304]{0:T(1024)}, f32[768]{0:T(1024)}, f32[3072]{0:T(1024)}, /*index=5*/f32[768]{0:T(1024)}, f3...) while((s32[]{:T(128)}, f32[256,768]{1,0:T(8,128)S(1)}, ...), condition=%wide.region_24.25_spmd.clone, body=%wide.region_7.24_spmd.clone.sunk | while | flops 5827556864 | bytes 286111680 | solution.py:374
  660.7 35.3 %fusion.260 = bf16[12,64,1024]{2,1,0:T(8,128)(2,1)} fusion(f32[12,256,1024]{2,1,0:T(8,128)} %fusion.259, f32[12,256,1024]{2,1,0:T(8,128)} %fusion.256, f32[12,256]{1,0:T(8,128)S(1)} %select_bitcast_fusion.3, pred[256,1024]{1,0:T(8,128)(4,1)} %broadcast_compare_fusion.5, bf16[3,256,12,64]{1,3,2,0:T(8,128)(2,1)} %get-tuple-element.2337, ...), kind=kOutput, calls=%fused_computation.133.clone.1 | convolution fusion | flops 447680512 | bytes 53249028 | tf_op jit(solution)/shard_map/while/body/eval_jaxpr/hqk,qhd->khd/dot_general | solution.py:198
  703.7 30.0 %fusion.261 = f32[256,12,64]{0,2,1:T(8,128)} fusion(f32[12,256,1024]{2,1,0:T(8,128)} %fusion.259, f32[12,256,1024]{2,1,0:T(8,128)} %fusion.256, f32[12,256]{1,0:T(8,128)S(1)} %select_bitcast_fusion.3, pred[256,1024]{1,0:T(8,128)(4,1)} %broadcast_compare_fusion.5, bf16[3,1024,12,64]{1,3,2,0:T(8,128)(2,1)} %get-tuple-element.2335, ...), kind=kOutput, calls=%fused_computation.149.clone.1 | convolution fusion | flops 447877120 | bytes 54821892 | tf_op jit(solution)/shard_map/while/body/eval_jaxpr/hqk,khd->qhd/dot_general | solution.py:195
  802.0 35.3 %fusion.260 = bf16[12,64,1024]{2,1,0:T(8,128)(2,1)} fusion(f32[12,256,1024]{2,1,0:T(8,128)} %fusion.259, f32[12,256,1024]{2,1,0:T(8,128)} %fusion.256, f32[12,256]{1,0:T(8,128)S(1)} %select_bitcast_fusion.3, pred[256,1024]{1,0:T(8,128)(4,1)} %broadcast_compare_fusion.5, bf16[3,256,12,64]{1,3,2,0:T(8,128)(2,1)} %get-tuple-element.2337, ...), kind=kOutput, calls=%fused_computation.133.clone.1 | convolution fusion | flops 447680512 | bytes 53249028 | tf_op jit(solution)/shard_map/while/body/eval_jaxpr/hqk,qhd->khd/dot_general | solution.py:198
  845.0 29.9 %fusion.261 = f32[256,12,64]{0,2,1:T(8,128)} fusion(f32[12,256,1024]{2,1,0:T(8,128)} %fusion.259, f32[12,256,1024]{2,1,0:T(8,128)} %fusion.256, f32[12,256]{1,0:T(8,128)S(1)} %select_bitcast_fusion.3, pred[256,1024]{1,0:T(8,128)(4,1)} %broadcast_compare_fusion.5, bf16[3,1024,12,64]{1,3,2,0:T(8,128)(2,1)} %get-tuple-element.2335, ...), kind=kOutput, calls=%fused_computation.149.clone.1 | convolution fusion | flops 447877120 | bytes 54821892 | tf_op jit(solution)/shard_map/while/body/eval_jaxpr/hqk,khd->qhd/dot_general | solution.py:195
  943.4 35.3 %fusion.260 = bf16[12,64,1024]{2,1,0:T(8,128)(2,1)} fusion(f32[12,256,1024]{2,1,0:T(8,128)} %fusion.259, f32[12,256,1024]{2,1,0:T(8,128)} %fusion.256, f32[12,256]{1,0:T(8,128)S(1)} %select_bitcast_fusion.3, pred[256,1024]{1,0:T(8,128)(4,1)} %broadcast_compare_fusion.5, bf16[3,256,12,64]{1,3,2,0:T(8,128)(2,1)} %get-tuple-element.2337, ...), kind=kOutput, calls=%fused_computation.133.clone.1 | convolution fusion | flops 447680512 | bytes 53249028 | tf_op jit(solution)/shard_map/while/body/eval_jaxpr/hqk,qhd->khd/dot_general | solution.py:198
  986.4 29.9 %fusion.261 = f32[256,12,64]{0,2,1:T(8,128)} fusion(f32[12,256,1024]{2,1,0:T(8,128)} %fusion.259, f32[12,256,1024]{2,1,0:T(8,128)} %fusion.256, f32[12,256]{1,0:T(8,128)S(1)} %select_bitcast_fusion.3, pred[256,1024]{1,0:T(8,128)(4,1)} %broadcast_compare_fusion.5, bf16[3,1024,12,64]{1,3,2,0:T(8,128)(2,1)} %get-tuple-element.2335, ...), kind=kOutput, calls=%fused_computation.149.clone.1 | convolution fusion | flops 447877120 | bytes 54821892 | tf_op jit(solution)/shard_map/while/body/eval_jaxpr/hqk,khd->qhd/dot_general | solution.py:195
  1097.8 63.8 %reduce-scatter.28.cloned.1.call-done = bf16[1,192,2304]{2,1,0:T(8,128)(2,1)} async-done(((bf16[1,768,2304]{2,1,0:T(8,128)(2,1)}), bf16[1,192,2304]{2,1,0:T(8,128)(2,1)}) %reduce-scatter.28.cloned.1.call-update) | async-done | bytes 884752 | tf_op jit(solution)/shard_map/reduce_scatter | solution.py:424
  1161.5 87.9 %reduce-scatter.34.cloned.1.call-done = bf16[1,768,768]{2,1,0:T(8,128)(2,1)} async-done(((bf16[1,3072,768]{2,1,0:T(8,128)(2,1)}), bf16[1,768,768]{2,1,0:T(8,128)(2,1)}) %reduce-scatter.34.cloned.1.call-update) | async-done | bytes 1179664 | tf_op jit(solution)/shard_map/reduce_scatter | solution.py:424
  1249.4 88.0 %reduce-scatter.32.cloned.1.call-done = bf16[1,192,3072]{2,1,0:T(8,128)(2,1)} async-done(((bf16[1,768,3072]{2,1,0:T(8,128)(2,1)}), bf16[1,192,3072]{2,1,0:T(8,128)(2,1)}) %reduce-scatter.32.cloned.1.call-update) | async-done | bytes 1179664 | tf_op jit(solution)/shard_map/reduce_scatter | solution.py:424
  1339.6 20.5 %reduce-scatter.38.cloned.1.call-done = bf16[192,1]{1,0:T(8,128)(2,1)} async-done(((bf16[768,1]{1,0:T(8,128)(2,1)}), bf16[192,1]{1,0:T(8,128)(2,1)}) %reduce-scatter.38.cloned.1.call-update) | async-done | bytes 400
  1361.0 19.6 %reduce-scatter.42.cloned.1.call-done = bf16[192,1]{1,0:T(8,128)(2,1)} async-done(((bf16[768,1]{1,0:T(8,128)(2,1)}), bf16[192,1]{1,0:T(8,128)(2,1)}) %reduce-scatter.42.cloned.1.call-update) | async-done | bytes 400
  1381.5 19.0 %reduce-scatter.44.cloned.1.call-done = bf16[192,1]{1,0:T(8,128)(2,1)} async-done(((bf16[768,1]{1,0:T(8,128)(2,1)}), bf16[192,1]{1,0:T(8,128)(2,1)}) %reduce-scatter.44.cloned.1.call-update) | async-done | bytes 400
  1441.1 22.2 %reduce-scatter.36.cloned.1.call-done = bf16[576,1]{1,0:T(8,128)(2,1)} async-done(((bf16[2304,1]{1,0:T(8,128)(2,1)}), bf16[576,1]{1,0:T(8,128)(2,1)}) %reduce-scatter.36.cloned.1.call-update) | async-done | bytes 1168
  1464.3 23.5 %reduce-scatter.40.cloned.1.call-done = bf16[768,1]{1,0:T(8,128)(2,1)} async-done(((bf16[3072,1]{1,0:T(8,128)(2,1)}), bf16[768,1]{1,0:T(8,128)(2,1)}) %reduce-scatter.40.cloned.1.call-update) | async-done | bytes 1552
  1508.6 76.7 %all-reduce.12.cloned.1.call-done = (bf16[1,192,2304]{2,1,0:T(8,128)(2,1)}, bf16[1,192,768]{2,1,0:T(8,128)(2,1)}, bf16[1,192,3072]{2,1,0:T(8,128)(2,1)}, bf16[1,768,768]{2,1,0:T(8,128)(2,1)}) async-done(((bf16[1,192,2304]{2,1,0:T(8,128)(2,1)}, bf16[1,192,768]{2,1,0:T(8,128)(2,1)}, bf16[1,192,3072]{2,1,0:T(8,128)(2,1)}, bf16[1,768,768]{2,1,0:T(8,128)(2,1)}), (bf16[1,192,2304]{2,1,0:T(8,128)(2,1)}, ...) | async-done | bytes 3538960 | tf_op jit(solution)/shard_map/psum | solution.py:432
  (794 shorter events, 611.8 us)
Async XLA Ops:
  8.0 106.6 %all-gather.7.cloned.1.call-start = ((), (), s32[]{:S(2)}) async-start(), calls=%async_computation.13 | async-start | bytes 4423680 | tf_op jit(solution)/shard_map/all_gather | solution.py:287
  8.8 195.4 %all-gather.11.cloned.1.call-start = ((), (), s32[]{:S(2)}) async-start(), calls=%async_computation.15 | async-start | bytes 5898240 | tf_op jit(solution)/shard_map/all_gather | solution.py:291
  9.5 284.0 %all-gather.13.cloned.1.call-start = ((), (), s32[]{:S(2)}) async-start(), calls=%async_computation.16 | async-start | bytes 5898240 | tf_op jit(solution)/shard_map/all_gather | solution.py:293
  321.5 62.9 %all-gather.15.cloned.1.call-start = ((), (), s32[]{:S(2)}) async-start(), calls=%async_computation.29 | async-start | bytes 1966080 | tf_op jit(solution)/shard_map/while/body/eval_jaxpr/all_gather | solution.py:108
  402.7 51.0 %all-gather.17.cloned.1.call-start = ((), (), s32[]{:S(2)}) async-start(), calls=%async_computation.30 | async-start | bytes 1966080 | tf_op jit(solution)/shard_map/while/body/eval_jaxpr/all_gather | solution.py:107
  422.8 64.6 %all-gather.15.cloned.1.call-start = ((), (), s32[]{:S(2)}) async-start(), calls=%async_computation.29 | async-start | bytes 1966080 | tf_op jit(solution)/shard_map/while/body/eval_jaxpr/all_gather | solution.py:108
  525.8 64.4 %all-gather.15.cloned.1.call-start = ((), (), s32[]{:S(2)}) async-start(), calls=%async_computation.29 | async-start | bytes 1966080 | tf_op jit(solution)/shard_map/while/body/eval_jaxpr/all_gather | solution.py:108
  636.6 123.1 %reduce-scatter.52.cloned.1.call-start = ((), (), s32[]{:S(2)}) async-start(), calls=%async_computation.32 | async-start | bytes 1966080 | tf_op jit(solution)/shard_map/while/body/eval_jaxpr/reduce_scatter | solution.py:205
  696.0 67.8 %reduce-scatter.50.cloned.1.call-start = ((), (), s32[]{:S(2)}) async-start(), calls=%async_computation.31 | async-start | bytes 1966080 | tf_op jit(solution)/shard_map/while/body/eval_jaxpr/reduce_scatter | solution.py:208
  777.9 123.0 %reduce-scatter.52.cloned.1.call-start = ((), (), s32[]{:S(2)}) async-start(), calls=%async_computation.32 | async-start | bytes 1966080 | tf_op jit(solution)/shard_map/while/body/eval_jaxpr/reduce_scatter | solution.py:205
  837.3 67.8 %reduce-scatter.50.cloned.1.call-start = ((), (), s32[]{:S(2)}) async-start(), calls=%async_computation.31 | async-start | bytes 1966080 | tf_op jit(solution)/shard_map/while/body/eval_jaxpr/reduce_scatter | solution.py:208
  919.3 123.1 %reduce-scatter.52.cloned.1.call-start = ((), (), s32[]{:S(2)}) async-start(), calls=%async_computation.32 | async-start | bytes 1966080 | tf_op jit(solution)/shard_map/while/body/eval_jaxpr/reduce_scatter | solution.py:205
  978.7 67.8 %reduce-scatter.50.cloned.1.call-start = ((), (), s32[]{:S(2)}) async-start(), calls=%async_computation.31 | async-start | bytes 1966080 | tf_op jit(solution)/shard_map/while/body/eval_jaxpr/reduce_scatter | solution.py:208
  1064.8 96.8 %reduce-scatter.28.cloned.1.call-start = ((), (), s32[]{:S(2)}) async-start(), calls=%async_computation.17 | async-start | bytes 4423680 | tf_op jit(solution)/shard_map/reduce_scatter | solution.py:424
  1071.3 178.1 %reduce-scatter.34.cloned.1.call-start = ((), (), s32[]{:S(2)}) async-start(), calls=%async_computation.20 | async-start | bytes 5898240 | tf_op jit(solution)/shard_map/reduce_scatter | solution.py:424
  1080.5 256.8 %reduce-scatter.32.cloned.1.call-start = ((), (), s32[]{:S(2)}) async-start(), calls=%async_computation.19 | async-start | bytes 5898240 | tf_op jit(solution)/shard_map/reduce_scatter | solution.py:424
  1089.8 270.3 %reduce-scatter.38.cloned.1.call-start = ((), (), s32[]{:S(2)}) async-start(), calls=%async_computation.22 | async-start | bytes 245760
  1091.3 289.3 %reduce-scatter.42.cloned.1.call-start = ((), (), s32[]{:S(2)}) async-start(), calls=%async_computation.24 | async-start | bytes 245760
  1092.2 308.3 %reduce-scatter.44.cloned.1.call-start = ((), (), s32[]{:S(2)}) async-start(), calls=%async_computation.25 | async-start | bytes 245760
  1093.1 327.2 %reduce-scatter.46.cloned.1.call-start = ((), (), s32[]{:S(2)}) async-start(), calls=%async_computation.26 | async-start | bytes 245760
  1094.1 346.1 %reduce-scatter.48.cloned.1.call-start = ((), (), s32[]{:S(2)}) async-start(), calls=%async_computation.27 | async-start | bytes 245760
  1095.0 368.3 %reduce-scatter.36.cloned.1.call-start = ((), (), s32[]{:S(2)}) async-start(), calls=%async_computation.21 | async-start | bytes 737280
  1096.3 391.5 %reduce-scatter.40.cloned.1.call-start = ((), (), s32[]{:S(2)}) async-start(), calls=%async_computation.23 | async-start | bytes 983040
  1097.7 487.6 %all-reduce.12.cloned.1.call-start = ((), (), s32[]{:S(2)}) async-start(), calls=%async_computation.28 | async-start | bytes 7077888 | tf_op jit(solution)/shard_map/psum | solution.py:432
  (173 other events, 1825.1 us)
Sparse Core Ops, SparseCore 0:
  9.7 34.2 all-gather.8
  45.5 69.0 all-gather.6
  116.2 87.9 all-gather.10
  205.6 87.8 all-gather.12
  321.6 29.2 all-gather.16
  353.4 30.9 all-gather.14
  422.9 30.8 all-gather.16
  456.3 31.0 all-gather.14
  525.9 30.8 all-gather.16
  559.2 30.9 all-gather.14
  696.1 30.9 reduce-scatter.51
  730.8 30.9 reduce-scatter.49
  837.5 31.1 reduce-scatter.51
  872.3 30.9 reduce-scatter.49
  978.8 31.1 reduce-scatter.51
  1013.7 30.9 reduce-scatter.49
  1064.9 29.3 reduce-scatter.29
  1096.5 65.0 reduce-scatter.27
  1163.8 85.5 reduce-scatter.33
  1251.5 85.7 reduce-scatter.31
  1340.2 19.8 reduce-scatter.37
  1443.0 20.2 reduce-scatter.35
  1466.1 21.5 reduce-scatter.39
  1491.6 93.6 all-reduce.11
  (4 shorter events, 70.1 us)
where the time goes:
time: 1610 us; the launch traced here: 1600 us
  waiting for transfers between devices  769 us (48%)
  matrix products  442 us (27%)
  other arithmetic  153 us (10%)
  local copies, waits for them, and re-layouts  125 us (8%)
  blocking collectives  51.3 us (3%)
  loops' own time  33.3 us (2%)
  between operations  16.4 us (1%)
    reduce_scatter x4, waiting for transfers between devices, per_device(): lax.psum_scatter(shortened(tuple((total[None] for total in totals))), 'ws...  240 us
    unnamed x23, waiting for transfers between devices  146 us
    dot_general x3, matrix products, layer_back(): jnp.einsum('hqk,qhd->khd', scaled_low, queries, preferred_element_type=jn...  106 us
    dot_general x3, matrix products, layer_back(): jnp.einsum('hqk,khd->qhd', scaled_low, all_keys, preferred_element_type=j...  89.8 us
    all_gather x1, waiting for transfers between devices, per_device(): lax.all_gather(shards[4], 'wshard', axis=1, tiled=True)  89.6 us
    all_gather x1, waiting for transfers between devices, per_device(): lax.all_gather(shards[6], 'wshard', axis=1, tiled=True)  89.3 us
    psum x1, waiting for transfers between devices, per_device(): lax.psum(shortened(summed), 'ctx')  76.7 us
    all_gather x1, waiting for transfers between devices, per_device(): lax.all_gather(shards[0], 'wshard', axis=1, tiled=True)  65.3 us
  transfers between devices with their start and end apart: 34, of which 22 were waited for; matrix products, arithmetic and copies ran while one was open for 24% of the time, Pallas kernels for 0%

commit v1 on v0

v1 whole, which is shorter than its diff:
```python
import math

import jax
import jax.numpy as jnp
from jax import lax
from jax.experimental import pallas as pl
from jax.experimental.pallas import tpu as pltpu
from jax.sharding import PartitionSpec as P

D = 768
H = 12
HD = 64
FF = 3072
ROT = 16
EPSILON = 1e-05
F32 = jnp.float32
BF16 = jnp.bfloat16
PAIRS = H * HD // 128
VMEM_LIMIT = 48 * 1024 * 1024


def dot_t(left, right):
    return lax.dot_general(left, right, (((1,), (1,)), ((), ())), preferred_element_type=F32)


def t_dot(left, right):
    return lax.dot_general(left, right, (((0,), (0,)), ((), ())), preferred_element_type=F32)


def dot(left, right):
    return jnp.dot(left, right, preferred_element_type=F32)


def swapped(part):
    return lax.ppermute(part, "section", [(0, 1), (1, 0)])


def positions(order_row, block_rows):
    return jnp.repeat(order_row, block_rows) * block_rows + jnp.tile(
        jnp.arange(block_rows, dtype=jnp.int32), order_row.shape[0]
    )


def turn_tables(places):
    half = ROT // 2
    frequency = jnp.exp(
        jnp.arange(half, dtype=F32) * F32(-2.0 * math.log(10000.0) / ROT)
    )
    angle = places.astype(F32)[:, None] * frequency[None, :]
    cosine, sine = jnp.cos(angle), jnp.sin(angle)
    rows = places.shape[0]
    ones = jnp.ones((rows, HD - ROT), F32)
    blank = jnp.zeros((rows, HD - half), F32)
    gap = jnp.zeros((rows, half), F32)
    tail = jnp.zeros((rows, HD - ROT), F32)
    cos_head = jnp.concatenate([cosine, cosine, ones], axis=1)
    low_head = jnp.concatenate([-sine, blank], axis=1)
    high_head = jnp.concatenate([gap, sine, tail], axis=1)
    return tuple(
        jnp.concatenate([table, table], axis=1) for table in (cos_head, low_head, high_head)
    )


def turned(values, cos_t, low_t, high_t, sign):
    half = ROT // 2
    ahead = pltpu.roll(values, 128 - half, 1)
    behind = pltpu.roll(values, half, 1)
    return values * cos_t + sign * (ahead * low_t + behind * high_t)


def rotate_kernel(k_ref, v_ref, cos_ref, low_ref, high_ref, out_ref):
    out_ref[0] = turned(k_ref[...], cos_ref[...], low_ref[...], high_ref[...], 1.0).astype(BF16)
    out_ref[1] = v_ref[...].astype(BF16)


def rotate_keys(projected_kv, tables):
    rows = projected_kv.shape[0]
    table = pl.BlockSpec((rows, 128), lambda h: (0, 0))
    return pl.pallas_call(
        rotate_kernel,
        grid=(PAIRS,),
        in_specs=[
            pl.BlockSpec((rows, 128), lambda h: (0, h)),
            pl.BlockSpec((rows, 128), lambda h: (0, PAIRS + h)),
            table,
            table,
            table,
        ],
        out_specs=pl.BlockSpec((2, rows, 128), lambda h: (0, 0, h)),
        out_shape=jax.ShapeDtypeStruct((2, rows, D), BF16),
        compiler_params=pltpu.CompilerParams(vmem_limit_bytes=VMEM_LIMIT),
        name="rotate_keys",
    )(projected_kv, projected_kv, *tables)


def attend_kernel(
    q_ref, kv_ref, cos_ref, low_ref, high_ref, all_ref, own_ref, mixed_ref, query_ref, stat_ref
):
    query = turned(q_ref[...], cos_ref[...], low_ref[...], high_ref[...], 1.0).astype(BF16)
    query_ref[...] = query
    visible = all_ref[...] <= own_ref[...]
    outs = []
    for head in range(2):
        lanes = slice(head * HD, (head + 1) * HD)
        keys, values = kv_ref[0, :, lanes], kv_ref[1, :, lanes]
        scores = jnp.where(visible, dot_t(keys, query[:, lanes]) * 0.125, -1e30)
        top = jnp.max(scores, axis=0, keepdims=True)
        weights = jnp.exp(scores - top)
        total = jnp.sum(weights, axis=0, keepdims=True)
        probs = (weights * (1.0 / total)).astype(BF16)
        outs.append(t_dot(values, probs))
        stat_ref[0, head : head + 1, :] = top + jnp.log(total)
    mixed_ref[...] = jnp.concatenate(outs, axis=0).T.astype(BF16)


def attend(projected_q, key_values, own_tables, places_all, places_own):
    rows, total = projected_q.shape[0], key_values.shape[1]
    table = pl.BlockSpec((rows, 128), lambda h: (0, 0))
    block = pl.BlockSpec((rows, 128), lambda h: (0, h))
    return pl.pallas_call(
        attend_kernel,
        grid=(PAIRS,),
        in_specs=[
            block,
            pl.BlockSpec((2, total, 128), lambda h: (0, 0, h)),
            table,
            table,
            table,
            pl.BlockSpec((total, 1), lambda h: (0, 0)),
            pl.BlockSpec((1, rows), lambda h: (0, 0)),
        ],
        out_specs=[block, block, pl.BlockSpec((1, 2, rows), lambda h: (h, 0, 0))],
        out_shape=[
            jax.ShapeDtypeStruct((rows, D), BF16),
            jax.ShapeDtypeStruct((rows, D), BF16),
            jax.ShapeDtypeStruct((PAIRS, 2, rows), F32),
        ],
        compiler_params=pltpu.CompilerParams(vmem_limit_bytes=VMEM_LIMIT),
        name="attend",
        cost_estimate=pl.CostEstimate(
            flops=4 * rows * total * D * 2, bytes_accessed=8 * total * D, transcendentals=rows * total * H
        ),
    )(projected_q, key_values, *own_tables, places_all[:, None], places_own[None, :])


def attend_back_kernel(
    query_ref, kv_ref, grad_ref, stat_ref,
    cos_ref, low_ref, high_ref, cos_all_ref, low_all_ref, high_all_ref,
    all_ref, own_ref, gq_ref, gkv_ref,
):
    visible = all_ref[...] <= own_ref[...]
    gq, gk, gv = [], [], []
    for head in range(2):
        lanes = slice(head * HD, (head + 1) * HD)
        keys, values = kv_ref[0, :, lanes], kv_ref[1, :, lanes]
        query, grad = query_ref[:, lanes], grad_ref[:, lanes]
        scores = dot_t(keys, query) * 0.125
        probs = jnp.where(visible, jnp.exp(scores - stat_ref[0, head : head + 1, :]), 0.0)
        grad_probs = dot_t(values, grad)
        delta = jnp.sum(probs * grad_probs, axis=0, keepdims=True)
        grad_scores = (probs * (grad_probs - delta)).astype(BF16)
        gq.append(t_dot(keys, grad_scores))
        gk.append(dot(grad_scores, query))
        gv.append(dot(probs.astype(BF16), grad))
    grad_query = (jnp.concatenate(gq, axis=0).T * 0.125).astype(BF16).astype(F32)
    gq_ref[...] = turned(
        grad_query, cos_ref[...], low_ref[...], high_ref[...], -1.0
    ).astype(BF16)
    grad_key = jnp.concatenate(gk, axis=1) * 0.125
    gkv_ref[0] = turned(
        grad_key, cos_all_ref[...], low_all_ref[...], high_all_ref[...], -1.0
    ).astype(BF16)
    gkv_ref[1] = jnp.concatenate(gv, axis=1).astype(BF16)


def attend_back(query, key_values, grad_mixed, stats, own_tables, all_tables, places_all, places_own):
    rows, total = query.shape[0], key_values.shape[1]
    table = pl.BlockSpec((rows, 128), lambda h: (0, 0))
    table_all = pl.BlockSpec((total, 128), lambda h: (0, 0))
    block = pl.BlockSpec((rows, 128), lambda h: (0, h))
    both = pl.BlockSpec((2, total, 128), lambda h: (0, 0, h))
    return pl.pallas_call(
        attend_back_kernel,
        grid=(PAIRS,),
        in_specs=[
            block, both, block, pl.BlockSpec((1, 2, rows), lambda h: (h, 0, 0)),
            table, table, table, table_all, table_all, table_all,
            pl.BlockSpec((total, 1), lambda h: (0, 0)),
            pl.BlockSpec((1, rows), lambda h: (0, 0)),
        ],
        out_specs=[block, both],
        out_shape=[
            jax.ShapeDtypeStruct((rows, D), BF16),
            jax.ShapeDtypeStruct((2, total, D), BF16),
        ],
        compiler_params=pltpu.CompilerParams(vmem_limit_bytes=VMEM_LIMIT),
        name="attend_back",
        cost_estimate=pl.CostEstimate(
            flops=10 * rows * total * D * 2, bytes_accessed=12 * total * D, transcendentals=rows * total * H
        ),
    )(
        query, key_values, grad_mixed, stats, *own_tables, *all_tables,
        places_all[:, None], places_own[None, :],
    )


def layer_forward(current, weights, geometry):
    (w_qkv, b_qkv, w_out, b_out, w_up, b_up, w_down, b_down, gain_a, shift_a, gain_m, shift_m) = weights
    own_tables, all_tables, places_all, places_own = geometry
    center = current - jnp.mean(current, axis=-1, keepdims=True)
    scale = lax.rsqrt(jnp.mean(center * center, axis=-1, keepdims=True) + EPSILON)
    normal = center * scale
    normed_a = (normal * gain_a + shift_a).astype(BF16)
    normed_m = (normal * gain_m + shift_m).astype(BF16)
    projected_kv = dot(normed_a, w_qkv[:, D:]) + b_qkv[D:]
    own_kv = rotate_keys(projected_kv, own_tables)
    key_values = lax.all_gather(own_kv, "ctx", axis=1, tiled=True)
    projected_q = dot(normed_a, w_qkv[:, :D]) + b_qkv[:D]
    pre = dot(normed_m, w_up) + b_up
    active = (pre * (1.0 + lax.erf(pre * F32(math.sqrt(0.5)))) * 0.5).astype(BF16)
    mlp_branch = dot(active, w_down) + b_down
    mixed, query, stats = attend(projected_q, key_values, own_tables, places_all, places_own)
    attn_branch = dot(mixed, w_out) + b_out
    result = (current + attn_branch + mlp_branch).astype(BF16)
    return result, (normal, scale, normed_a, normed_m, query, key_values, stats, mixed, pre, active)


def layer_backward(weights, geometry, grad_low, kept):
    (w_qkv, b_qkv, w_out, b_out, w_up, b_up, w_down, b_down, gain_a, shift_a, gain_m, shift_m) = weights
    own_tables, all_tables, places_all, places_own = geometry
    normal, scale, normed_a, normed_m, query, key_values, stats, mixed, pre, active = kept
    grad_out = grad_low.astype(F32)
    grad_mixed = dot_t(grad_low, w_out).astype(BF16)
    grad_q, grad_kv_all = attend_back(
        query, key_values, grad_mixed, stats, own_tables, all_tables, places_all, places_own
    )
    grad_kv = lax.psum_scatter(grad_kv_all, "ctx", scatter_dimension=1, tiled=True)
    grad_active = dot_t(grad_low, w_down)
    slope = 0.5 * (1.0 + lax.erf(pre * F32(math.sqrt(0.5)))) + pre * jnp.exp(
        -0.5 * pre * pre
    ) * F32(1.0 / math.sqrt(2.0 * math.pi))
    grad_pre = (grad_active * slope).astype(BF16)
    grad_normed_m = dot_t(grad_pre, w_up)
    grad_projected = jnp.concatenate([grad_q, grad_kv[0], grad_kv[1]], axis=1)
    grad_normed_a = dot_t(grad_projected, w_qkv)
    through = grad_normed_a * gain_a + grad_normed_m * gain_m
    grad_input = (
        grad_out
        + scale
        * (
            through
            - jnp.mean(through, axis=-1, keepdims=True)
            - normal * jnp.mean(through * normal, axis=-1, keepdims=True)
        )
    ).astype(BF16)
    pairs = (
        (normed_a, grad_projected),
        (mixed, grad_low),
        (normed_m, grad_pre),
        (active, grad_low),
    )
    sums = (
        jnp.sum(grad_projected.astype(F32), axis=0),
        jnp.sum(grad_out, axis=0),
        jnp.sum(grad_pre.astype(F32), axis=0),
        jnp.sum(grad_normed_a * normal, axis=0),
        jnp.sum(grad_normed_a, axis=0),
        jnp.sum(grad_normed_m * normal, axis=0),
        jnp.sum(grad_normed_m, axis=0),
    )
    return grad_input, pairs, sums


def half_of(wide, index):
    width = wide.shape[1] // 2
    return lax.dynamic_slice_in_dim(wide, index * width, width, 1)


def weight_terms(pairs, section):
    done = []
    for left, right in pairs:
        left_both = jnp.concatenate([left, swapped(left)], axis=0)
        right_both = jnp.concatenate(
            [half_of(right, section), swapped(half_of(right, 1 - section))], axis=0
        )
        done.append(t_dot(left_both, right_both).astype(BF16))
    return done


def folded(tall, chunks):
    rows, width = tall.shape[0] // (4 * chunks), tall.shape[1]
    blocks = tall.reshape(chunks, 4, rows, width)
    return jnp.transpose(blocks, (0, 2, 1, 3)).reshape(chunks * rows, 4 * width)


def unfolded(flat, chunks):
    rows, width = flat.shape[0] // chunks, flat.shape[1] // 4
    blocks = flat.reshape(chunks, rows, 4, width)
    return jnp.transpose(blocks, (0, 2, 1, 3)).reshape(chunks * 4 * rows, width)


def padded(thin):
    return jnp.pad(thin, ((0, 0), (0, 128 - thin.shape[1])))


def per_device(
    tokens, cotangent, block_map, w_qkv, b_qkv, w_out, b_out, w_up, b_up, w_down, b_down,
    gain_attn, shift_attn, gain_mlp, shift_mlp,
):
    section = lax.axis_index("section")
    first = section == 0
    ctx_count = lax.axis_size("ctx")
    shards_n = lax.axis_size("wshard")
    rows = tokens.shape[1]

    def pick(stacked):
        return lax.dynamic_index_in_dim(stacked, section, 0, keepdims=False)

    own_tokens, own_cotangent, order_row = pick(tokens), pick(cotangent), pick(block_map)
    block_rows = rows * ctx_count // order_row.shape[0]
    places_all = positions(order_row, block_rows)
    start = lax.axis_index("ctx") * rows
    all_tables = turn_tables(places_all)
    places_own = lax.dynamic_slice_in_dim(places_all, start, rows, 0)
    own_tables = tuple(lax.dynamic_slice_in_dim(table, start, rows, 0) for table in all_tables)
    geometry = (own_tables, all_tables, places_all, places_own)

    small = (b_qkv, b_out, b_up, b_down, gain_attn, shift_attn, gain_mlp, shift_mlp)
    widths = [vector.shape[1] for vector in small]
    part_rows = w_qkv.shape[1] // ctx_count
    chunks = shards_n * ctx_count
    thin_width = sum(widths) // w_qkv.shape[1]

    def part_of(shard):
        count = shard.shape[0] // ctx_count
        return lax.dynamic_slice_in_dim(shard, lax.axis_index("ctx") * count, count, 0)

    def gathered(parts):
        joined = jnp.concatenate(parts, axis=1)
        return lax.all_gather(joined, ("section", "wshard", "ctx"), axis=0, tiled=True).reshape(
            2, chunks * part_rows, -1
        )

    vector_rows = part_of(jnp.concatenate(small, axis=1)[0].reshape(-1, thin_width))
    both_a = gathered([part_of(w_qkv[0]), part_of(w_out[0]), padded(vector_rows)])
    both_b = gathered([part_of(w_up[0]), folded(part_of(w_down[0]), 1)])
    packed = both_a[:, :, 4 * D : 4 * D + thin_width].reshape(2, shards_n, -1)
    vectors, at = [], 0
    for width in widths:
        vectors.append(packed[:, :, at : at + width].reshape(2, -1).astype(F32))
        at += width

    def layer_weights(j):
        qkv, out = both_a[j, :, : 3 * D], both_a[j, :, 3 * D : 4 * D]
        up, down = both_b[j, :, :FF], unfolded(both_b[j, :, FF:], chunks)
        (v_qkv, v_out, v_up, v_down, g_a, s_a, g_m, s_m) = (vector[j] for vector in vectors)
        return (qkv, v_qkv, out, v_out, up, v_up, down, v_down, g_a, s_a, g_m, s_m)

    lower, upper = layer_weights(0), layer_weights(1)
    middle, kept_lower = layer_forward(own_tokens.astype(F32), lower, geometry)
    final, kept_upper = layer_forward(middle.astype(F32), upper, geometry)
    grad_middle, pairs_upper, sums_upper = layer_backward(upper, geometry, own_cotangent, kept_upper)
    upper_terms = weight_terms(pairs_upper, section)
    grad_input, pairs_lower, sums_lower = layer_backward(lower, geometry, grad_middle, kept_lower)
    lower_terms = weight_terms(pairs_lower, section)

    def together(low_part, high_part):
        own = jnp.where(first, low_part, high_part)
        other = swapped(jnp.where(first, high_part, low_part))
        return jnp.where(first, own, other), jnp.where(first, other, own)

    outputs = jnp.stack(together(middle, final))[None]
    boundary = jnp.stack(together(grad_input, grad_middle))[None].astype(F32)

    def packed_terms(terms, sums):
        t_qkv, t_out, t_up, t_down = terms
        g_qkv, g_bias, g_up, g_ga, g_sa, g_gm, g_sm = (part.reshape(shards_n, -1) for part in sums)
        shard_sums = jnp.concatenate([g_qkv, g_bias, g_up, g_bias, g_ga, g_sa, g_gm, g_sm], axis=1)
        thin = padded(shard_sums.astype(BF16).reshape(-1, thin_width))
        return [t_qkv, t_out, t_up, folded(t_down, chunks), thin]

    everything = jnp.concatenate(
        packed_terms(lower_terms, sums_lower) + packed_terms(upper_terms, sums_upper), axis=1
    )
    summed = lax.psum_scatter(everything, ("wshard", "ctx"), scatter_dimension=0, tiled=True)
    low_part, high_part = jnp.split(summed, 2, axis=1)
    own = jnp.where(first, low_part, high_part)
    other = swapped(jnp.where(first, high_part, low_part))
    left, right = jnp.where(first, own, other), jnp.where(first, other, own)
    cuts = [(0, 3 * D // 2), (3 * D // 2, 2 * D), (2 * D, 2 * D + FF // 2)]
    columns = [piece[:, lo:hi] for lo, hi in cuts for piece in (left, right)]
    base = 2 * D + FF // 2
    for k in range(4):
        at = base + k * (D // 2)
        columns += [left[:, at : at + D // 2], right[:, at : at + D // 2]]
    at = base + 2 * D
    columns.append((left[:, at:].astype(F32) + right[:, at:].astype(F32)).astype(BF16))
    shard = lax.all_gather(jnp.concatenate(columns, axis=1), "ctx", axis=0, tiled=True).astype(F32)
    ends = [0, 3 * D, 4 * D, 4 * D + FF]
    grads = [shard[:, lo:hi][None] for lo, hi in zip(ends[:-1], ends[1:])]
    at = 4 * D + FF
    grads.append(unfolded(shard[:, at : at + 4 * D], ctx_count)[None])
    at += 4 * D
    own_sums = shard[:, at : at + thin_width].reshape(1, -1)
    vector_grads, at = [], 0
    for width in widths:
        vector_grads.append(own_sums[:, at : at + width])
        at += width
    s_qkv, s_out, s_up, s_down, s_ga, s_sa, s_gm, s_sm = vector_grads
    return (
        outputs, boundary, grads[0], s_qkv, grads[1], s_out, grads[2], s_up, grads[3], s_down,
        s_ga, s_sa, s_gm, s_sm,
    )


def solution(mesh):
    wide = P("section", "wshard", None)
    thin = P("section", "wshard")
    rows = P("wshard", "ctx", None)
    stacked = P("section", "wshard", "ctx", None)
    weights = (wide, thin) * 4 + (thin,) * 4
    return jax.shard_map(
        per_device, mesh=mesh, in_specs=(rows, rows, P("wshard", None)) + weights,
        out_specs=(stacked, stacked) + weights, check_vma=False,
    )
```

time: 1610 us -> 872 us (0.54)
  matrix products: 442 us -> 90 us
  waiting for transfers between devices: 769 us -> 561 us
  other arithmetic: 153 us -> 25.8 us
  Pallas kernels: 0 us -> 63.6 us
  blocking collectives: 51.3 us -> 0 us
  loops' own time: 33.3 us -> 0 us
  local copies, waits for them, and re-layouts: 125 us -> 104 us
    dot_general x49 -> x26, matrix products: 442 us -> 90 us  [the longest x8 32.9 us: dot_t(): lax.dot_general(left, right, (((1,), (1,)), ((), ())), preferred_element_...]
    unnamed x23 -> x8, waiting for transfers between devices: 146 us -> 0.13 us
    psum x1 -> x0, waiting for transfers between devices: 76.7 us -> none  [per_device(): lax.psum(shortened(summed), 'ctx')]
    pallas_call x0 -> x6, Pallas kernels: none -> 63.6 us  [the longest x2 32.5 us: attend_back(): pl.pallas_call(attend_back_kernel, grid=(PAIRS,), in_specs=[block, both,...]
    dynamic_update_slice x33 -> x0, other arithmetic: 48.9 us -> none  [the longest x30 45.6 us: per_device(): lax.scan(forward_turn, zero_rows, turns)]
    another operation x2 -> x0, loops' own time: 33.3 us -> none  [the longest x1 26.3 us: per_device(): lax.scan(backward_turn, (zero_rows, start_sums), turns)]
    dynamic_update_slice x18 -> x0, local copies, waits for them, and re-layouts: 27.5 us -> none  [per_device(): lax.scan(forward_turn, zero_rows, turns)]
    convert_element_type x57 -> x7, other arithmetic: 36.1 us -> 9.19 us  [the longest x2 3.2 us: layer_forward(): normed_a = (normal * gain_a + shift_a).astype(BF16)]
  transfers between devices with their start and end apart: 34 -> 25, of which waited for: 22 -> 10; matrix products, arithmetic and copies ran while one was open for 24% -> 13% of each run, Pallas kernels for 0% -> 1%
where the time goes in v1:
time: 872 us; the launch traced here: 865 us
  waiting for transfers between devices  561 us (64%)
  local copies, waits for them, and re-layouts  104 us (12%)
  matrix products  90 us (10%)
  Pallas kernels  63.6 us (7%)
  other arithmetic  25.8 us (3%)
  between operations  15.6 us (2%)
    reduce_scatter x1, waiting for transfers between devices, per_device(): lax.psum_scatter(everything, ('wshard', 'ctx'), scatter_dimension=0, tile...  225 us
    all_gather x2, waiting for transfers between devices, gathered(): lax.all_gather(joined, ('section', 'wshard', 'ctx'), axis=0, tiled=True)  186 us
    all_gather x2, waiting for transfers between devices, layer_forward(): key_values = lax.all_gather(own_kv, 'ctx', axis=1, tiled=True)  71.5 us
    all_gather x1, waiting for transfers between devices, per_device(): lax.all_gather(jnp.concatenate(columns, axis=1), 'ctx', axis=0, tiled=True)  42.6 us
    reduce_scatter x2, waiting for transfers between devices, layer_backward(): lax.psum_scatter(grad_kv_all, 'ctx', scatter_dimension=1, tiled=True)  33.9 us
    dot_general x8, matrix products, dot_t(): lax.dot_general(left, right, (((1,), (1,)), ((), ())), preferred_element_...  32.9 us
    pallas_call x2, Pallas kernels, attend_back(): pl.pallas_call(attend_back_kernel, grid=(PAIRS,), in_specs=[block, both,...  32.5 us
    dot_general x10, matrix products, dot(): return jnp.dot(left, right, preferred_element_type=F32)  29.7 us
  transfers between devices with their start and end apart: 25, of which 10 were waited for; matrix products, arithmetic and copies ran while one was open for 13% of the time, Pallas kernels for 1%

profile of v1, /device:TPU:0, one launch (start us, length us, event | category | flops | bytes accessed | tf_op | source)
XLA Modules:
  0.0 865.4 jit_solution(7854681166010920743)
XLA Ops:
  23.6 74.1 %all-gather.6.cloned.1.call-done = bf16[1536,3200]{1,0:T(8,128)(2,1)} async-done(((bf16[48,3200]{1,0:T(8,128)(2,1)}), bf16[1536,3200]{1,0:T(8,128)(2,1)}) %all-gather.6.cloned.1.call-update) | async-done | bytes 9830416 | tf_op jit(solution)/shard_map/all_gather | solution.py:340
  98.8 6.5 slice_bitcast_fusion.10
  123.3 35.0 %all-gather.8.cloned.1.call-done.kv_ref = bf16[2,1024,768]{2,1,0:T(8,128)(2,1)} async-done(((bf16[2,256,768]{2,1,0:T(8,128)(2,1)}), bf16[2,1024,768]{2,1,0:T(8,128)(2,1)}) %all-gather.8.cloned.1.call-update) | async-done | bytes 3145744 | tf_op jit(solution)/shard_map/all_gather | solution.py:217
  161.4 12.9 %attend.2 = (bf16[256,768]{1,0:T(8,128)(2,1)S(1)}, bf16[256,768]{1,0:T(8,128)(2,1)S(1)}, f32[6,2,256]{2,1,0:T(2,128)S(1)}) custom-call(f32[256,768]{1,0:T(8,128)S(1)} %copy-done.6, bf16[2,1024,768]{2,1,0:T(8,128)(2,1)S(1)} %copy-done.2, f32[256,128]{1,0:T(8,128)S(1)} %constant_dynamic-slice_fusion.13.cos_ref, f32[256,128]{1,0:T(8,128)S(1)} %get-tuple-element.145.low_ref, ...), custom_call_target="tpu_custom_call" | custom-call | flops 1610612736 | bytes 6291456 | tf_op jit(solution)/shard_map/attend/pallas_call | solution.py:120
  175.0 111.4 %all-gather.10.cloned.1.call-done = bf16[1536,6144]{1,0:T(8,128)(2,1)} async-done(((bf16[48,6144]{1,0:T(8,128)(2,1)}), bf16[1536,6144]{1,0:T(8,128)(2,1)}) %all-gather.10.cloned.1.call-update) | async-done | bytes 18874384 | tf_op jit(solution)/shard_map/all_gather | solution.py:340
  286.4 8.2 fusion.149
  294.6 9.8 %reshape_squeeze.10 = bf16[16,48,4,768]{3,2,1,0:T(4,128)(2,1)} reshape(bf16[1,768,3072]{2,1,0:T(8,128)(2,1)} %get-tuple-element.61) | data formatting | bytes 9437184 | tf_op jit(solution)/shard_map/reshape;squeeze | solution.py:298
  307.7 7.5 multiply_convert_fusion.1
  330.5 36.4 %all-gather.12.cloned.1.call-done.kv_ref = bf16[2,1024,768]{2,1,0:T(8,128)(2,1)} async-done(((bf16[2,256,768]{2,1,0:T(8,128)(2,1)}), bf16[2,1024,768]{2,1,0:T(8,128)(2,1)}) %all-gather.12.cloned.1.call-update) | async-done | bytes 3145744 | tf_op jit(solution)/shard_map/all_gather | solution.py:217
  370.0 12.9 %attend.3 = (bf16[256,768]{1,0:T(8,128)(2,1)S(1)}, bf16[256,768]{1,0:T(8,128)(2,1)S(1)}, f32[6,2,256]{2,1,0:T(2,128)S(1)}) custom-call(f32[256,768]{1,0:T(8,128)S(1)} %copy-done.7, bf16[2,1024,768]{2,1,0:T(8,128)(2,1)S(1)} %copy-done.3, f32[256,128]{1,0:T(8,128)S(1)} %constant_dynamic-slice_fusion.13.cos_ref, f32[256,128]{1,0:T(8,128)S(1)} %get-tuple-element.145.low_ref, ...), custom_call_target="tpu_custom_call" | custom-call | flops 1610612736 | bytes 6291456 | tf_op jit(solution)/shard_map/attend/pallas_call | solution.py:120
  382.9 16.3 %attend_back.2 = (bf16[256,768]{1,0:T(8,128)(2,1)S(1)}, bf16[2,1024,768]{2,1,0:T(8,128)(2,1)}) custom-call(bf16[256,768]{1,0:T(8,128)(2,1)S(1)} %get-tuple-element.26.query_ref, bf16[2,1024,768]{2,1,0:T(8,128)(2,1)} %all-gather.12.cloned.1.call-done.kv_ref, bf16[256,768]{1,0:T(8,128)(2,1)S(1)} %copy-done.8, f32[6,2,256]{2,1,0:T(2,128)S(1)} %get-tuple-element.27.stat_ref, ...), custom_call_target="tpu_custom_call" | custom-call | flops 4026531840 | bytes 9437184 | tf_op jit(solution)/shard_map/attend_back/pallas_call | solution.py:182
  399.4 9.9 %reshape_squeeze.11 = bf16[16,48,4,768]{3,2,1,0:T(4,128)(2,1)} reshape(bf16[1,768,3072]{2,1,0:T(8,128)(2,1)} %get-tuple-element.60) | data formatting | bytes 9437184 | tf_op jit(solution)/shard_map/reshape;squeeze | solution.py:298
  422.1 21.2 %reduce-scatter.4.cloned.1.call-done = bf16[2,256,768]{2,1,0:T(8,128)(2,1)} async-done(((bf16[2,1024,768]{2,1,0:T(8,128)(2,1)}), bf16[2,256,768]{2,1,0:T(8,128)(2,1)}) %reduce-scatter.4.cloned.1.call-update) | async-done | bytes 786448 | tf_op jit(solution)/shard_map/reduce_scatter | solution.py:237
  448.4 4.8 fusion.141
  458.0 16.2 %attend_back.3 = (bf16[256,768]{1,0:T(8,128)(2,1)S(1)}, bf16[2,1024,768]{2,1,0:T(8,128)(2,1)}) custom-call(bf16[256,768]{1,0:T(8,128)(2,1)S(1)} %copy-done.10, bf16[2,1024,768]{2,1,0:T(8,128)(2,1)} %all-gather.8.cloned.1.call-done.kv_ref, bf16[256,768]{1,0:T(8,128)(2,1)S(1)} %convolution_convert_fusion.8.grad_ref, ...), custom_call_target="tpu_custom_call" | custom-call | flops 4026531840 | bytes 9437184 | tf_op jit(solution)/shard_map/attend_back/pallas_call | solution.py:182
  487.9 7.4 fusion.158
  500.9 4.7 convolution_convert_fusion.1
  505.7 12.7 %reduce-scatter.6.cloned.1.call-done = bf16[2,256,768]{2,1,0:T(8,128)(2,1)} async-done(((bf16[2,1024,768]{2,1,0:T(8,128)(2,1)}), bf16[2,256,768]{2,1,0:T(8,128)(2,1)}) %reduce-scatter.6.cloned.1.call-update) | async-done | bytes 786448 | tf_op jit(solution)/shard_map/reduce_scatter | solution.py:237
  524.4 5.7 fusion.88
  538.3 4.1 fusion.11
  543.9 4.2 fusion.10
  550.5 3.9 fusion.9
  561.3 225.1 %reduce-scatter.8.cloned.1.call-done = bf16[48,9472]{1,0:T(8,128)(2,1)} async-done(((bf16[768,9472]{1,0:T(8,128)(2,1)}), bf16[48,9472]{1,0:T(8,128)(2,1)}) %reduce-scatter.8.cloned.1.call-update) | async-done | bytes 909328 | tf_op jit(solution)/shard_map/reduce_scatter | solution.py:385
  796.9 42.6 %all-gather.14.cloned.1.call-done = bf16[192,9344]{1,0:T(8,128)(2,1)} async-done(((bf16[48,9344]{1,0:T(8,128)(2,1)}), bf16[192,9344]{1,0:T(8,128)(2,1)}) %all-gather.14.cloned.1.call-update) | async-done | bytes 3588112 | tf_op jit(solution)/shard_map/all_gather | solution.py:398
  (371 shorter events, 156.2 us)
Async XLA Ops:
  7.2 90.5 %all-gather.6.cloned.1.call-start = ((), (), s32[]{:S(2)}) async-start(), calls=%async_computation.3 | async-start | bytes 10137600 | tf_op jit(solution)/shard_map/all_gather | solution.py:340
  11.1 147.2 %all-gather.8.cloned.1.call-start = ((), (), s32[]{:S(2)}) async-start(), calls=%async_computation.4 | async-start | bytes 3932160 | tf_op jit(solution)/shard_map/all_gather | solution.py:217
  115.6 170.8 %all-gather.10.cloned.1.call-start = ((), (), s32[]{:S(2)}) async-start(), calls=%async_computation.5 | async-start | bytes 19464192 | tf_op jit(solution)/shard_map/all_gather | solution.py:340
  117.8 249.2 %all-gather.12.cloned.1.call-start = ((), (), s32[]{:S(2)}) async-start(), calls=%async_computation.6 | async-start | bytes 3932160 | tf_op jit(solution)/shard_map/all_gather | solution.py:217
  324.7 118.6 %reduce-scatter.4.cloned.1.call-start = ((), (), s32[]{:S(2)}) async-start(), calls=%async_computation.7 | async-start | bytes 3932160 | tf_op jit(solution)/shard_map/reduce_scatter | solution.py:237
  399.2 119.2 %reduce-scatter.6.cloned.1.call-start = ((), (), s32[]{:S(2)}) async-start(), calls=%async_computation.8 | async-start | bytes 3932160 | tf_op jit(solution)/shard_map/reduce_scatter | solution.py:237
  474.3 312.1 %reduce-scatter.8.cloned.1.call-start = ((), (), s32[]{:S(2)}) async-start(), calls=%async_computation.9 | async-start | bytes 15458304 | tf_op jit(solution)/shard_map/reduce_scatter | solution.py:385
  474.5 5.4 collective-permute-start.15
  476.1 3.6 collective-permute-start.12
  477.6 60.1 %collective-permute-start.2 = (bf16[256,768]{1,0:T(8,128)(2,1)}, bf16[256,768]{1,0:T(8,128)(2,1)}, u32[]{:S(2)}, u32[]{:S(2)}) collective-permute-start(bf16[256,768]{1,0:T(8,128)(2,1)} %fusion.79), channel_id=1, source_target_pairs={{0,16},{16,0},{1,17},{17,1},{2,18},{18,2},{3,19},{19,3},{4,20},{20... | collective-permute-start | bytes 1179656 | tf_op jit(solution)/shard_map/ppermute | solution.py:35
  477.8 52.3 %collective-permute-start.4 = (bf16[256,768]{1,0:T(8,128)(2,1)S(1)}, bf16[256,768]{1,0:T(8,128)(2,1)}, u32[]{:S(2)}, u32[]{:S(2)}) collective-permute-start(bf16[256,768]{1,0:T(8,128)(2,1)S(1)} %copy-done.5), channel_id=1, source_target_pairs={{0,16},{16,0},{1,17},{17,1},{2,18},{18,2},{3,19},{19,3},{4,20},{20... | collective-permute-start | bytes 1179656 | tf_op jit(solution)/shard_map/ppermute | solution.py:35
  478.1 22.7 %collective-permute-start.8 = (bf16[256,3072]{1,0:T(8,128)(2,1)}, bf16[256,3072]{1,0:T(8,128)(2,1)}, u32[]{:S(2)}, u32[]{:S(2)}) collective-permute-start(bf16[256,3072]{1,0:T(8,128)(2,1)} %copy-done.71), channel_id=1, source_target_pairs={{0,16},{16,0},{1,17},{17,1},{2,18},{18,2},{3,19},{19,3},{4,20},{20... | collective-permute-start | bytes 4718600 | tf_op jit(solution)/shard_map/ppermute | solution.py:35
  479.6 70.9 %collective-permute-start.9 = (bf16[256,768]{1,0:T(8,128)(2,1)}, bf16[256,768]{1,0:T(8,128)(2,1)}, u32[]{:S(2)}, u32[]{:S(2)}) collective-permute-start(bf16[256,768]{1,0:T(8,128)(2,1)} %get-tuple-element.90), channel_id=1, source_target_pairs={{0,16},{16,0},{1,17},{17,1},{2,18},{18,2},{3,19},{19,3},{4,20},{20... | collective-permute-start | bytes 1179656 | tf_op jit(solution)/shard_map/ppermute | solution.py:35
  486.9 14.0 %collective-permute-start.5 = (bf16[256,384]{1,0:T(8,128)(2,1)S(1)}, bf16[256,384]{1,0:T(8,128)(2,1)S(1)}, u32[]{:S(2)}, u32[]{:S(2)}) collective-permute-start(bf16[256,384]{1,0:T(8,128)(2,1)S(1)} %get-tuple-element.93), channel_id=1, source_target_pairs={{0,16},{16,0},{1,17},{17,1},{2,18},{18,2},{3,19},{19,3},{4,20},{20... | collective-permute-start | bytes 589832 | tf_op jit(solution)/shard_map/ppermute | solution.py:35
  500.8 42.5 %collective-permute-start.7 = (bf16[256,1536]{1,0:T(8,128)(2,1)}, bf16[256,1536]{1,0:T(8,128)(2,1)}, u32[]{:S(2)}, u32[]{:S(2)}) collective-permute-start(bf16[256,1536]{1,0:T(8,128)(2,1)} %get-tuple-element.67), channel_id=1, source_target_pairs={{0,16},{16,0},{1,17},{17,1},{2,18},{18,2},{3,19},{19,3},{4,20},{20... | collective-permute-start | bytes 2359304 | tf_op jit(solution)/shard_map/ppermute | solution.py:35
  524.3 13.6 %collective-permute-start.3 = (bf16[256,1152]{1,0:T(8,128)(2,1)}, bf16[256,1152]{1,0:T(8,128)(2,1)}, u32[]{:S(2)}, u32[]{:S(2)}) collective-permute-start(bf16[256,1152]{1,0:T(8,128)(2,1)} %get-tuple-element.78), channel_id=1, source_target_pairs={{0,16},{16,0},{1,17},{17,1},{2,18},{18,2},{3,19},{19,3},{4,20},{20... | collective-permute-start | bytes 1769480 | tf_op jit(solution)/shard_map/ppermute | solution.py:35
  530.1 13.4 %collective-permute-start.6 = (bf16[256,768]{1,0:T(8,128)(2,1)}, bf16[256,768]{1,0:T(8,128)(2,1)}, u32[]{:S(2)}, u32[]{:S(2)}) collective-permute-start(bf16[256,768]{1,0:T(8,128)(2,1)} %get-tuple-element.83), channel_id=1, source_target_pairs={{0,16},{16,0},{1,17},{17,1},{2,18},{18,2},{3,19},{19,3},{4,20},{20... | collective-permute-start | bytes 1179656 | tf_op jit(solution)/shard_map/ppermute | solution.py:35
  537.7 18.2 %collective-permute-start.13 = (bf16[256,768]{1,0:T(8,128)(2,1)}, bf16[256,768]{1,0:T(8,128)(2,1)S(1)}, u32[]{:S(2)}, u32[]{:S(2)}) collective-permute-start(bf16[256,768]{1,0:T(8,128)(2,1)} %get-tuple-element.91), channel_id=1, source_target_pairs={{0,16},{16,0},{1,17},{17,1},{2,18},{18,2},{3,19},{19,3},{4,20},{20... | collective-permute-start | bytes 1179656 | tf_op jit(solution)/shard_map/ppermute | solution.py:35
  537.9 18.0 %collective-permute-start.14 = (bf16[256,1536]{1,0:T(8,128)(2,1)}, bf16[256,1536]{1,0:T(8,128)(2,1)S(1)}, u32[]{:S(2)}, u32[]{:S(2)}) collective-permute-start(bf16[256,1536]{1,0:T(8,128)(2,1)} %get-tuple-element.65), channel_id=1, source_target_pairs={{0,16},{16,0},{1,17},{17,1},{2,18},{18,2},{3,19},{19,3},{4,20},{20... | collective-permute-start | bytes 2359304 | tf_op jit(solution)/shard_map/ppermute | solution.py:35
  543.4 11.1 %collective-permute-start.11 = (bf16[256,768]{1,0:T(8,128)(2,1)S(1)}, bf16[256,768]{1,0:T(8,128)(2,1)S(1)}, u32[]{:S(2)}, u32[]{:S(2)}) collective-permute-start(bf16[256,768]{1,0:T(8,128)(2,1)S(1)} %get-tuple-element.25), channel_id=1, source_target_pairs={{0,16},{16,0},{1,17},{17,1},{2,18},{18,2},{3,19},{19,3},{4,20},{20... | collective-permute-start | bytes 1179656 | tf_op jit(solution)/shard_map/ppermute | solution.py:35
  543.5 7.0 collective-permute-start.10
  561.3 278.2 %all-gather.14.cloned.1.call-start = ((), (), s32[]{:S(2)}) async-start(), calls=%async_computation.10 | async-start | bytes 4485120 | tf_op jit(solution)/shard_map/all_gather | solution.py:398
  787.6 1.9 collective-permute-start.16
  792.0 2.2 collective-permute-start
  (81 other events, 2370.9 us)
Sparse Core Ops, SparseCore 0:
  11.5 86.1 all-gather.5
  115.8 42.5 all-gather.7
  161.8 124.5 all-gather.9
  324.8 42.1 all-gather.11
  399.3 43.9 reduce-scatter.3
  474.4 43.8 reduce-scatter.5
  561.4 225.0 reduce-scatter.7
  792.1 47.2 all-gather.13
